TPU v7x, 32 devices: a whole 2x2x4 slice. The times are simulated.
32 devices in a mesh: loop: 8 (over y, x, core), group: 4 (over z).
Axes of the slice: x: 2, y: 2, z: 4, core: 2. Of those that a mesh axis runs over, the one named last changes fastest.
Arguments:
- embeddings: bfloat16 [4096, 1024], P(('loop', 'group')), may hold values from -8 to 8
- partner: int32 [4096], P(('loop', 'group')), may hold values from 0 to 4095, as said below
Outputs:
- loss: float32 [], replicated
- log_norm: float32 [4096], P(('loop', 'group'))
- grad: float32 [4096, 1024], P(('loop', 'group'))
Inputs may be any that keep to these rules, and one draw needn't show every extreme that they name: partner[partner[i]] = i and partner[i] != i for every view i.
All inputs are finite; a program needn't handle non-finite values.
Results may differ from a plain program's by a relative error of at most 0.0022.
Values may be sent and summed in bfloat16 or wider, within the bound.
A program may use at most 64 MiB of HBM per device.

v0:
```python
import math

import jax
import jax.numpy as jnp
from jax import lax
from jax.sharding import PartitionSpec as P

MASKED = -1e30


def shifted(value, axis, by):
    length = lax.axis_size(axis)
    return lax.ppermute(value, axis, [(i, (i + by) % length) for i in range(length)])


def circulate(update, running, shared):
    cycle_len = lax.axis_size("loop")
    position = lax.axis_index("loop")
    running = update(running, shared, position)

    def advance(k, bundle):
        status, visitor = bundle
        visitor = shifted(visitor, "loop", 1)
        return (update(status, visitor, (position - k) % cycle_len), visitor)

    running, _ = lax.fori_loop(1, cycle_len, advance, (running, shared))
    return running


def per_device(embeddings, partner):
    rows_here = embeddings.shape[0]
    width = embeddings.shape[1]
    cycle_len = lax.axis_size("loop")
    groups = lax.axis_size("group")
    block_rows = rows_here * groups
    views = block_rows * cycle_len
    scale = 1.0 / math.sqrt(width)
    position = lax.axis_index("loop")
    member = lax.axis_index("group")
    row_ids = (position * groups + member) * rows_here + jnp.arange(rows_here, dtype=jnp.int32)
    shared = lax.all_gather(embeddings, "group", axis=0, tiled=True)

    def scores_with(visitor, root):
        col_ids = root * block_rows + jnp.arange(block_rows, dtype=jnp.int32)
        scores = (
            lax.dot_general(
                embeddings, visitor, (((1,), (1,)), ((), ())), preferred_element_type=jnp.float32
            )
            * scale
        )
        scores = jnp.where(row_ids[:, None] == col_ids[None, :], jnp.float32(MASKED), scores)
        return (scores, col_ids)

    def first_update(running, visitor, root):
        scores, col_ids = scores_with(visitor, root)
        new_peak = jnp.maximum(running[0], jnp.max(scores, axis=1))
        mass = running[1] * jnp.exp(running[0] - new_peak) + jnp.sum(
            jnp.exp(scores - new_peak[:, None]), axis=1
        )
        positive = running[2] + jnp.sum(
            jnp.where(partner[:, None] == col_ids[None, :], scores, jnp.float32(0.0)), axis=1
        )
        return (new_peak, mass, positive)

    start_peak = jnp.full((rows_here,), MASKED, jnp.float32)
    start_zero = jnp.zeros((rows_here,), jnp.float32)
    peak, mass, positive = circulate(first_update, (start_peak, start_zero, start_zero), shared)
    log_norm = peak + jnp.log(mass)
    all_norms = lax.all_gather(log_norm, ("loop", "group"), axis=0, tiled=True)
    loss = lax.psum(jnp.sum(log_norm - positive), ("loop", "group")) / views

    def second_update(total, visitor, root):
        scores, col_ids = scores_with(visitor, root)
        col_norms = lax.dynamic_slice_in_dim(all_norms, root * block_rows, block_rows, 0)
        weights = jnp.exp(scores - log_norm[:, None]) + jnp.exp(scores - col_norms[None, :])
        weights = weights - 2.0 * (partner[:, None] == col_ids[None, :]).astype(jnp.float32)
        return total + jnp.dot(
            weights.astype(jnp.bfloat16), visitor, preferred_element_type=jnp.float32
        )

    zeros = jnp.zeros((rows_here, width), jnp.float32)
    total = circulate(second_update, zeros, shared)
    return (loss, log_norm, total * scale)


def solution(mesh):
    placed = (P(("loop", "group"), None), P(("loop", "group")))
    return jax.shard_map(
        per_device,
        mesh=mesh,
        in_specs=placed,
        out_specs=(P(), P(("loop", "group")), P(("loop", "group"), None)),
        check_vma=False,
    )
```

profile of v0, /device:TPU:0, one launch (start us, length us, event | category | flops | bytes accessed | tf_op | source)
XLA Modules:
  0.0 386.6 jit_solution(978210452835532642)
XLA Ops:
  7.9 32.3 %all-gather.3.cloned.1.call-done = bf16[512,1024]{1,0:T(8,128)(2,1)} async-done(((bf16[128,1024]{1,0:T(8,128)(2,1)}), bf16[512,1024]{1,0:T(8,128)(2,1)}) %all-gather.3.cloned.1.call-update) | async-done | bytes 1048592 | tf_op jit(solution)/shard_map/all_gather | solution.py:41
  40.2 1.8 fusion.36
  42.9 1.2 copy-done.2
  44.2 112.6 %while.40 = (s32[]{:T(128)}, f32[128]{0:T(128)S(1)}, f32[128]{0:T(128)S(1)}, f32[128]{0:T(128)S(1)}, bf16[512,1024]{1,0:T(8,128)(2,1)S(1)}, /*index=5*/s32[]{:T(...) while((s32[]{:T(128)}, f32[128]{0:T(128)S(1)}, ...), condition=%wide.region_7.8_spmd.clone, body=%wide.region_3.7_spmd.clone.sunk | while | flops 134808464 | bytes 8143162 | solution.py:26
  44.2 15.1 %collective-permute-done = bf16[512,1024]{1,0:T(8,128)(2,1)S(1)} collective-permute-done((bf16[512,1024]{1,0:T(8,128)(2,1)S(1)}, bf16[512,1024]{1,0:T(8,128)(2,1)S(1)}, u32[]{:S(2)}, u32[]{:S(2)}) %collective-permute-start) | collective-permute-done | bytes 1048608 | tf_op jit(solution)/shard_map/while/body/eval_jaxpr/ppermute | solution.py:13
  60.3 15.1 %collective-permute-done = bf16[512,1024]{1,0:T(8,128)(2,1)S(1)} collective-permute-done((bf16[512,1024]{1,0:T(8,128)(2,1)S(1)}, bf16[512,1024]{1,0:T(8,128)(2,1)S(1)}, u32[]{:S(2)}, u32[]{:S(2)}) %collective-permute-start) | collective-permute-done | bytes 1048608 | tf_op jit(solution)/shard_map/while/body/eval_jaxpr/ppermute | solution.py:13
  76.4 15.1 %collective-permute-done = bf16[512,1024]{1,0:T(8,128)(2,1)S(1)} collective-permute-done((bf16[512,1024]{1,0:T(8,128)(2,1)S(1)}, bf16[512,1024]{1,0:T(8,128)(2,1)S(1)}, u32[]{:S(2)}, u32[]{:S(2)}) %collective-permute-start) | collective-permute-done | bytes 1048608 | tf_op jit(solution)/shard_map/while/body/eval_jaxpr/ppermute | solution.py:13
  92.5 15.1 %collective-permute-done = bf16[512,1024]{1,0:T(8,128)(2,1)S(1)} collective-permute-done((bf16[512,1024]{1,0:T(8,128)(2,1)S(1)}, bf16[512,1024]{1,0:T(8,128)(2,1)S(1)}, u32[]{:S(2)}, u32[]{:S(2)}) %collective-permute-start) | collective-permute-done | bytes 1048608 | tf_op jit(solution)/shard_map/while/body/eval_jaxpr/ppermute | solution.py:13
  108.6 15.1 %collective-permute-done = bf16[512,1024]{1,0:T(8,128)(2,1)S(1)} collective-permute-done((bf16[512,1024]{1,0:T(8,128)(2,1)S(1)}, bf16[512,1024]{1,0:T(8,128)(2,1)S(1)}, u32[]{:S(2)}, u32[]{:S(2)}) %collective-permute-start) | collective-permute-done | bytes 1048608 | tf_op jit(solution)/shard_map/while/body/eval_jaxpr/ppermute | solution.py:13
  124.7 15.1 %collective-permute-done = bf16[512,1024]{1,0:T(8,128)(2,1)S(1)} collective-permute-done((bf16[512,1024]{1,0:T(8,128)(2,1)S(1)}, bf16[512,1024]{1,0:T(8,128)(2,1)S(1)}, u32[]{:S(2)}, u32[]{:S(2)}) %collective-permute-start) | collective-permute-done | bytes 1048608 | tf_op jit(solution)/shard_map/while/body/eval_jaxpr/ppermute | solution.py:13
  140.8 15.1 %collective-permute-done = bf16[512,1024]{1,0:T(8,128)(2,1)S(1)} collective-permute-done((bf16[512,1024]{1,0:T(8,128)(2,1)S(1)}, bf16[512,1024]{1,0:T(8,128)(2,1)S(1)}, u32[]{:S(2)}, u32[]{:S(2)}) %collective-permute-start) | collective-permute-done | bytes 1048608 | tf_op jit(solution)/shard_map/while/body/eval_jaxpr/ppermute | solution.py:13
  157.4 39.4 %psum.7 = f32[]{:T(128)} all-reduce(f32[]{:T(128)} %get-tuple-element.533), channel_id=1, replica_groups=mesh['loop'=8,'group'=4] {'loop','group'}, use_global_device_ids=true, to_apply=%region_9.10 | all-reduce | flops 1 | bytes 8 | tf_op jit(solution)/shard_map/psum | solution.py:70
  196.8 65.5 %all-gather = f32[32,1,128]{2,1,0:T(1,128)S(1)} all-gather(f32[1,1,128]{2,1,0:T(1,128)S(1)} %bitcast.22), channel_id=1, replica_groups=mesh['loop'=8,'group'=4] {'loop','group'}, dimensions={0}, use_global_device_ids=true | all-gather | bytes 16896 | tf_op jit(solution)/shard_map/all_gather | solution.py:69
  262.4 1.6 fusion.25
  264.0 112.6 %while.41 = (s32[]{:T(128)}, f32[128,1024]{1,0:T(8,128)S(1)}, bf16[512,1024]{1,0:T(8,128)(2,1)S(1)}, s32[]{:T(128)}, bf16[128,1024]{1,0:T(8,128)(2,1)S(1)}, /*in...) while((s32[]{:T(128)}, f32[128,1024]{1,0:T(8,128)S(1)}, ...), condition=%wide.region_11.12_spmd.clone, body=%wide.region_10.11_spmd.clone.sunk | while | flops 269222560 | bytes 8663400 | solution.py:26
  264.2 15.0 %collective-permute-done.1 = bf16[512,1024]{1,0:T(8,128)(2,1)S(1)} collective-permute-done((bf16[512,1024]{1,0:T(8,128)(2,1)S(1)}, bf16[512,1024]{1,0:T(8,128)(2,1)S(1)}, u32[]{:S(2)}, u32[]{:S(2)}) %collective-permute-start.1) | collective-permute-done | bytes 1048608 | tf_op jit(solution)/shard_map/while/body/eval_jaxpr/ppermute | solution.py:13
  279.3 0.8 convolution_add_fusion.2
  280.3 15.0 %collective-permute-done.1 = bf16[512,1024]{1,0:T(8,128)(2,1)S(1)} collective-permute-done((bf16[512,1024]{1,0:T(8,128)(2,1)S(1)}, bf16[512,1024]{1,0:T(8,128)(2,1)S(1)}, u32[]{:S(2)}, u32[]{:S(2)}) %collective-permute-start.1) | collective-permute-done | bytes 1048608 | tf_op jit(solution)/shard_map/while/body/eval_jaxpr/ppermute | solution.py:13
  296.3 15.0 %collective-permute-done.1 = bf16[512,1024]{1,0:T(8,128)(2,1)S(1)} collective-permute-done((bf16[512,1024]{1,0:T(8,128)(2,1)S(1)}, bf16[512,1024]{1,0:T(8,128)(2,1)S(1)}, u32[]{:S(2)}, u32[]{:S(2)}) %collective-permute-start.1) | collective-permute-done | bytes 1048608 | tf_op jit(solution)/shard_map/while/body/eval_jaxpr/ppermute | solution.py:13
  312.4 15.0 %collective-permute-done.1 = bf16[512,1024]{1,0:T(8,128)(2,1)S(1)} collective-permute-done((bf16[512,1024]{1,0:T(8,128)(2,1)S(1)}, bf16[512,1024]{1,0:T(8,128)(2,1)S(1)}, u32[]{:S(2)}, u32[]{:S(2)}) %collective-permute-start.1) | collective-permute-done | bytes 1048608 | tf_op jit(solution)/shard_map/while/body/eval_jaxpr/ppermute | solution.py:13
  328.5 15.0 %collective-permute-done.1 = bf16[512,1024]{1,0:T(8,128)(2,1)S(1)} collective-permute-done((bf16[512,1024]{1,0:T(8,128)(2,1)S(1)}, bf16[512,1024]{1,0:T(8,128)(2,1)S(1)}, u32[]{:S(2)}, u32[]{:S(2)}) %collective-permute-start.1) | collective-permute-done | bytes 1048608 | tf_op jit(solution)/shard_map/while/body/eval_jaxpr/ppermute | solution.py:13
  344.6 15.0 %collective-permute-done.1 = bf16[512,1024]{1,0:T(8,128)(2,1)S(1)} collective-permute-done((bf16[512,1024]{1,0:T(8,128)(2,1)S(1)}, bf16[512,1024]{1,0:T(8,128)(2,1)S(1)}, u32[]{:S(2)}, u32[]{:S(2)}) %collective-permute-start.1) | collective-permute-done | bytes 1048608 | tf_op jit(solution)/shard_map/while/body/eval_jaxpr/ppermute | solution.py:13
  360.7 15.0 %collective-permute-done.1 = bf16[512,1024]{1,0:T(8,128)(2,1)S(1)} collective-permute-done((bf16[512,1024]{1,0:T(8,128)(2,1)S(1)}, bf16[512,1024]{1,0:T(8,128)(2,1)S(1)}, u32[]{:S(2)}, u32[]{:S(2)}) %collective-permute-start.1) | collective-permute-done | bytes 1048608 | tf_op jit(solution)/shard_map/while/body/eval_jaxpr/ppermute | solution.py:13
  377.1 0.8 broadcast_multiply_fusion
  (129 shorter events, 15.8 us)
Async XLA Ops:
  7.2 33.1 %copy-start = (bf16[128,1024]{1,0:T(8,128)(2,1)S(1)}, bf16[128,1024]{1,0:T(8,128)(2,1)}, u32[]{:S(2)}) copy-start(bf16[128,1024]{1,0:T(8,128)(2,1)} %param.6) | copy-start | bytes 786436
  7.2 33.1 %all-gather.3.cloned.1.call-start = ((), (), s32[]{:S(2)}) async-start(), calls=%async_computation | async-start | bytes 1310720 | tf_op jit(solution)/shard_map/all_gather | solution.py:41
  42.0 0.7 copy-start.3
  42.9 1.2 copy-start.2
  44.2 15.1 %collective-permute-start = (bf16[512,1024]{1,0:T(8,128)(2,1)S(1)}, bf16[512,1024]{1,0:T(8,128)(2,1)S(1)}, u32[]{:S(2)}, u32[]{:S(2)}) collective-permute-start(bf16[512,1024]{1,0:T(8,128)(2,1)S(1)} %get-tuple-element.675), channel_id=1, source_target_pairs={{0,4},{4,8},{8,12},{12,16},{16,20},{20,24},{24,28},{28,0},{1,5},{5... | collective-permute-start | bytes 3145736 | tf_op jit(solution)/shard_map/while/body/eval_jaxpr/ppermute | solution.py:13
  60.2 15.2 %collective-permute-start = (bf16[512,1024]{1,0:T(8,128)(2,1)S(1)}, bf16[512,1024]{1,0:T(8,128)(2,1)S(1)}, u32[]{:S(2)}, u32[]{:S(2)}) collective-permute-start(bf16[512,1024]{1,0:T(8,128)(2,1)S(1)} %get-tuple-element.675), channel_id=1, source_target_pairs={{0,4},{4,8},{8,12},{12,16},{16,20},{20,24},{24,28},{28,0},{1,5},{5... | collective-permute-start | bytes 3145736 | tf_op jit(solution)/shard_map/while/body/eval_jaxpr/ppermute | solution.py:13
  76.3 15.2 %collective-permute-start = (bf16[512,1024]{1,0:T(8,128)(2,1)S(1)}, bf16[512,1024]{1,0:T(8,128)(2,1)S(1)}, u32[]{:S(2)}, u32[]{:S(2)}) collective-permute-start(bf16[512,1024]{1,0:T(8,128)(2,1)S(1)} %get-tuple-element.675), channel_id=1, source_target_pairs={{0,4},{4,8},{8,12},{12,16},{16,20},{20,24},{24,28},{28,0},{1,5},{5... | collective-permute-start | bytes 3145736 | tf_op jit(solution)/shard_map/while/body/eval_jaxpr/ppermute | solution.py:13
  92.4 15.2 %collective-permute-start = (bf16[512,1024]{1,0:T(8,128)(2,1)S(1)}, bf16[512,1024]{1,0:T(8,128)(2,1)S(1)}, u32[]{:S(2)}, u32[]{:S(2)}) collective-permute-start(bf16[512,1024]{1,0:T(8,128)(2,1)S(1)} %get-tuple-element.675), channel_id=1, source_target_pairs={{0,4},{4,8},{8,12},{12,16},{16,20},{20,24},{24,28},{28,0},{1,5},{5... | collective-permute-start | bytes 3145736 | tf_op jit(solution)/shard_map/while/body/eval_jaxpr/ppermute | solution.py:13
  108.5 15.2 %collective-permute-start = (bf16[512,1024]{1,0:T(8,128)(2,1)S(1)}, bf16[512,1024]{1,0:T(8,128)(2,1)S(1)}, u32[]{:S(2)}, u32[]{:S(2)}) collective-permute-start(bf16[512,1024]{1,0:T(8,128)(2,1)S(1)} %get-tuple-element.675), channel_id=1, source_target_pairs={{0,4},{4,8},{8,12},{12,16},{16,20},{20,24},{24,28},{28,0},{1,5},{5... | collective-permute-start | bytes 3145736 | tf_op jit(solution)/shard_map/while/body/eval_jaxpr/ppermute | solution.py:13
  124.6 15.2 %collective-permute-start = (bf16[512,1024]{1,0:T(8,128)(2,1)S(1)}, bf16[512,1024]{1,0:T(8,128)(2,1)S(1)}, u32[]{:S(2)}, u32[]{:S(2)}) collective-permute-start(bf16[512,1024]{1,0:T(8,128)(2,1)S(1)} %get-tuple-element.675), channel_id=1, source_target_pairs={{0,4},{4,8},{8,12},{12,16},{16,20},{20,24},{24,28},{28,0},{1,5},{5... | collective-permute-start | bytes 3145736 | tf_op jit(solution)/shard_map/while/body/eval_jaxpr/ppermute | solution.py:13
  140.7 15.2 %collective-permute-start = (bf16[512,1024]{1,0:T(8,128)(2,1)S(1)}, bf16[512,1024]{1,0:T(8,128)(2,1)S(1)}, u32[]{:S(2)}, u32[]{:S(2)}) collective-permute-start(bf16[512,1024]{1,0:T(8,128)(2,1)S(1)} %get-tuple-element.675), channel_id=1, source_target_pairs={{0,4},{4,8},{8,12},{12,16},{16,20},{20,24},{24,28},{28,0},{1,5},{5... | collective-permute-start | bytes 3145736 | tf_op jit(solution)/shard_map/while/body/eval_jaxpr/ppermute | solution.py:13
  156.8 107.2 %copy-start.1 = (bf16[512,1024]{1,0:T(8,128)(2,1)S(1)}, bf16[512,1024]{1,0:T(8,128)(2,1)}, u32[]{:S(2)}) copy-start(bf16[512,1024]{1,0:T(8,128)(2,1)} %all-gather.3.cloned.1.call-done) | copy-start | bytes 3145732
  264.0 15.2 %collective-permute-start.1 = (bf16[512,1024]{1,0:T(8,128)(2,1)S(1)}, bf16[512,1024]{1,0:T(8,128)(2,1)S(1)}, u32[]{:S(2)}, u32[]{:S(2)}) collective-permute-start(bf16[512,1024]{1,0:T(8,128)(2,1)S(1)} %get-tuple-element.716), channel_id=1, source_target_pairs={{0,4},{4,8},{8,12},{12,16},{16,20},{20,24},{24,28},{28,0},{1,5},{5... | collective-permute-start | bytes 3145736 | tf_op jit(solution)/shard_map/while/body/eval_jaxpr/ppermute | solution.py:13
  280.1 15.2 %collective-permute-start.1 = (bf16[512,1024]{1,0:T(8,128)(2,1)S(1)}, bf16[512,1024]{1,0:T(8,128)(2,1)S(1)}, u32[]{:S(2)}, u32[]{:S(2)}) collective-permute-start(bf16[512,1024]{1,0:T(8,128)(2,1)S(1)} %get-tuple-element.716), channel_id=1, source_target_pairs={{0,4},{4,8},{8,12},{12,16},{16,20},{20,24},{24,28},{28,0},{1,5},{5... | collective-permute-start | bytes 3145736 | tf_op jit(solution)/shard_map/while/body/eval_jaxpr/ppermute | solution.py:13
  296.2 15.2 %collective-permute-start.1 = (bf16[512,1024]{1,0:T(8,128)(2,1)S(1)}, bf16[512,1024]{1,0:T(8,128)(2,1)S(1)}, u32[]{:S(2)}, u32[]{:S(2)}) collective-permute-start(bf16[512,1024]{1,0:T(8,128)(2,1)S(1)} %get-tuple-element.716), channel_id=1, source_target_pairs={{0,4},{4,8},{8,12},{12,16},{16,20},{20,24},{24,28},{28,0},{1,5},{5... | collective-permute-start | bytes 3145736 | tf_op jit(solution)/shard_map/while/body/eval_jaxpr/ppermute | solution.py:13
  312.3 15.2 %collective-permute-start.1 = (bf16[512,1024]{1,0:T(8,128)(2,1)S(1)}, bf16[512,1024]{1,0:T(8,128)(2,1)S(1)}, u32[]{:S(2)}, u32[]{:S(2)}) collective-permute-start(bf16[512,1024]{1,0:T(8,128)(2,1)S(1)} %get-tuple-element.716), channel_id=1, source_target_pairs={{0,4},{4,8},{8,12},{12,16},{16,20},{20,24},{24,28},{28,0},{1,5},{5... | collective-permute-start | bytes 3145736 | tf_op jit(solution)/shard_map/while/body/eval_jaxpr/ppermute | solution.py:13
  328.3 15.2 %collective-permute-start.1 = (bf16[512,1024]{1,0:T(8,128)(2,1)S(1)}, bf16[512,1024]{1,0:T(8,128)(2,1)S(1)}, u32[]{:S(2)}, u32[]{:S(2)}) collective-permute-start(bf16[512,1024]{1,0:T(8,128)(2,1)S(1)} %get-tuple-element.716), channel_id=1, source_target_pairs={{0,4},{4,8},{8,12},{12,16},{16,20},{20,24},{24,28},{28,0},{1,5},{5... | collective-permute-start | bytes 3145736 | tf_op jit(solution)/shard_map/while/body/eval_jaxpr/ppermute | solution.py:13
  344.4 15.2 %collective-permute-start.1 = (bf16[512,1024]{1,0:T(8,128)(2,1)S(1)}, bf16[512,1024]{1,0:T(8,128)(2,1)S(1)}, u32[]{:S(2)}, u32[]{:S(2)}) collective-permute-start(bf16[512,1024]{1,0:T(8,128)(2,1)S(1)} %get-tuple-element.716), channel_id=1, source_target_pairs={{0,4},{4,8},{8,12},{12,16},{16,20},{20,24},{24,28},{28,0},{1,5},{5... | collective-permute-start | bytes 3145736 | tf_op jit(solution)/shard_map/while/body/eval_jaxpr/ppermute | solution.py:13
  360.5 15.2 %collective-permute-start.1 = (bf16[512,1024]{1,0:T(8,128)(2,1)S(1)}, bf16[512,1024]{1,0:T(8,128)(2,1)S(1)}, u32[]{:S(2)}, u32[]{:S(2)}) collective-permute-start(bf16[512,1024]{1,0:T(8,128)(2,1)S(1)} %get-tuple-element.716), channel_id=1, source_target_pairs={{0,4},{4,8},{8,12},{12,16},{16,20},{20,24},{24,28},{28,0},{1,5},{5... | collective-permute-start | bytes 3145736 | tf_op jit(solution)/shard_map/while/body/eval_jaxpr/ppermute | solution.py:13
  376.6 0.5 copy-start.4
Sparse Core Ops, SparseCore 0:
  9.6 30.6 all-gather.2
where the time goes:
time: 387 us
  waiting for transfers between devices  243 us (63%)
  blocking collectives  105 us (27%)
  between operations  16 us (4%)
  matrix products  13 us (3%)
  local copies, waits for them, and re-layouts  4 us (1%)
    ppermute x14, waiting for transfers between devices, shifted(): lax.ppermute(value, axis, [(i, (i + by) % length) for i in range(length)])  210 us
    all_gather x1, blocking collectives, per_device(): all_norms = lax.all_gather(log_norm, ('loop', 'group'), axis=0, tiled=True)  65.5 us
    psum x1, blocking collectives, per_device(): loss = lax.psum(jnp.sum(log_norm - positive), ('loop', 'group')) / views  39.4 us
    all_gather x1, waiting for transfers between devices, per_device(): shared = lax.all_gather(embeddings, 'group', axis=0, tiled=True)  32.3 us
  transfers between devices with their start and end apart: 15, of which 15 were waited for; matrix products, arithmetic and copies ran while one was open for 0% of the time, Pallas kernels for 0%

commit v1 on v0

v1 whole, which is shorter than its diff:
```python
import functools
import math

import jax
import jax.numpy as jnp
from jax import lax
from jax.experimental import pallas as pl
from jax.experimental.pallas import tpu as pltpu
from jax.sharding import PartitionSpec as P

MASKED = -1e30
MESH = pl.DeviceIdType.MESH


def kernel(
    loops, groups, emb_ref, prt_ref, loss_ref, norm_ref, grad_ref,
    all_e, scores, own_col, prt_col, stats,
    z_send, x_send, y_send, c_send, line_recv, part_recv, c_recv, barrier_free_send, stat_recv,
):
    l = lax.axis_index("loop")
    g = lax.axis_index("group")
    n = loops * groups
    ys = loops // 4
    rows, width = emb_ref.shape
    scale = 1.0 / math.sqrt(width)
    c = lax.rem(l, 2)
    x = lax.rem(l // 2, 2)
    y = l // 4
    me = l * groups + g

    def quad(xx, yy):
        return yy * 2 + xx

    def block(cc, q, z):
        return (q * 2 + cc) * groups + z

    def slot(q, z):
        return q * groups + z

    mine = quad(x, y)
    other_x = quad(1 - x, y)
    other_y = [quad(x, lax.rem(y + d, ys)) for d in range(1, ys)]
    other_xy = [quad(1 - x, lax.rem(y + d, ys)) for d in range(1, ys)]

    barrier = pltpu.get_barrier_semaphore()

    def greet(k, _):
        t = lax.rem(me + k, n)
        pl.semaphore_signal(
            barrier, inc=1, device_id=(t // groups, lax.rem(t, groups)), device_id_type=MESH
        )
        return 0

    lax.fori_loop(1, n, greet, 0)
    all_e[me] = emb_ref[...]
    pl.semaphore_wait(barrier, n - 1)

    pending = []

    def send(q, z, lo, size, send_sem, recv_sem, target, when=None):
        b = block(c, q, z)

        def make():
            part = all_e.at[b, pl.ds(lo, size)]
            return pltpu.make_async_remote_copy(
                src_ref=part, dst_ref=part, send_sem=send_sem, recv_sem=recv_sem,
                device_id=target, device_id_type=MESH,
            )

        def go():
            make().start()

        def done():
            make().wait_send()

        if when is None:
            go()
        else:
            pl.when(when)(go)
        pending.append((when, done))

    def arrived(q, z, lo, size, recv_sem, cc=None):
        part = all_e.at[block(c if cc is None else cc, q, z), pl.ds(lo, size)]
        pltpu.make_async_copy(part, part, recv_sem).wait()

    def both(a, b):
        return b if a is None else jnp.logical_and(a, b)

    def when_do(cond, fn):
        if cond is None:
            fn()
        else:
            pl.when(cond)(fn)

    def sides(k):
        if k == 0:
            return [(g, None, (1, -1))]
        return [(g + k, g + k < groups, (-1,)), (g - k, g - k >= 0, (1,))]

    half = rows // 2
    small = 16

    def to_z(q, z, lo, size, recv_sem, valid, steps):
        for step in steps:
            can = (g < groups - 1) if step == 1 else (g > 0)
            send(q, z, lo, size, z_send.at[slot(q, z), 0 if step == 1 else 1], recv_sem,
                 (l, g + step), both(valid, can))

    def to_sibling(q, z, valid):
        send(q, z, 0, rows, c_send.at[slot(q, z)], c_recv.at[slot(q, z)], (l + 1 - 2 * c, g), valid)

    def to_x(q, z, lo, size, recv_sem, valid):
        send(q, z, lo, size, x_send.at[slot(q, z)], recv_sem, (l + 2 - 4 * x, g), valid)

    def to_y(q, z, lo, size, recv_sem, valid):
        for d in range(1, ys):
            send(q, z, lo, size, y_send.at[slot(q, z), d - 1], recv_sem,
                 (lax.rem(y + d, ys) * 4 + x * 2 + c, g), valid)

    def own_line(k):
        for z, valid, steps in sides(k):
            s = slot(mine, z)
            if k > 0:
                when_do(valid, lambda: arrived(mine, z, 0, rows, line_recv.at[s]))
            to_z(mine, z, 0, rows, line_recv.at[s], valid, steps)
            to_x(mine, z, 0, rows, line_recv.at[s], valid)
            to_y(mine, z, 0, rows, line_recv.at[s], valid)
            to_sibling(mine, z, valid)

    def from_x(k):
        for z, valid, _ in sides(k):
            s = slot(other_x, z)
            when_do(valid, lambda: arrived(other_x, z, 0, rows, line_recv.at[s]))
            to_y(other_x, z, 0, half if k == 0 else small, part_recv.at[s, 0], valid)
            to_sibling(other_x, z, valid)

    def from_y(k):
        for z, valid, _ in sides(k):
            for q in other_y:
                s = slot(q, z)
                when_do(valid, lambda: arrived(q, z, 0, rows, line_recv.at[s]))
                if k == 0:
                    to_x(q, z, half, rows - half, part_recv.at[s, 1], valid)
                else:
                    to_x(q, z, small, small, part_recv.at[s, 1], valid)
                to_sibling(q, z, valid)

    def from_diagonal(k):
        for z, valid, steps in sides(k):
            for q in other_xy:
                s = slot(q, z)

                def wait_parts():
                    if k == 0:
                        arrived(q, z, 0, half, part_recv.at[s, 0])
                        arrived(q, z, half, rows - half, part_recv.at[s, 1])
                    else:
                        arrived(q, z, 2 * small, rows - 2 * small, line_recv.at[s])

                when_do(valid, wait_parts)
                to_z(q, z, 2 * small, rows - 2 * small, line_recv.at[s], valid, steps)
                if k > 0:
                    def wait_rest():
                        arrived(q, z, 0, small, part_recv.at[s, 0])
                        arrived(q, z, small, small, part_recv.at[s, 1])

                    when_do(valid, wait_rest)
                to_sibling(q, z, valid)

    row_iota = lax.broadcasted_iota(jnp.int32, (rows, rows), 0)
    col_iota = lax.broadcasted_iota(jnp.int32, (rows, rows), 1)

    def score(b):
        s = lax.dot_general(
            emb_ref[...], all_e[b], (((1,), (1,)), ((), ())), preferred_element_type=jnp.float32
        ) * scale
        masked = jnp.logical_and(row_iota == col_iota, b == me)
        scores[b] = jnp.where(masked, jnp.float32(MASKED), s)

    def score_own(k):
        for z, valid, _ in sides(k):
            def run():
                def body(q, _):
                    score(block(c, q, z))
                    return 0
                lax.fori_loop(0, loops // 2, body, 0)
            when_do(valid, run)

    def score_sibling(k):
        for z, valid, _ in sides(k):
            def run():
                def body(q, _):
                    arrived(q, z, 0, rows, c_recv.at[slot(q, z)], 1 - c)
                    score(block(1 - c, q, z))
                    return 0
                lax.fori_loop(0, loops // 2, body, 0)
            when_do(valid, run)

    own_line(0)
    prt = jnp.broadcast_to(prt_ref[...].astype(jnp.float32), (rows, rows))
    prt_col[...] = prt.T.astype(jnp.int32)
    if groups > 1:
        own_line(1)
    for k in range(groups):
        from_x(k)
        from_y(k)
        if k + 2 < groups:
            own_line(k + 2)
        from_diagonal(k)
        score_own(k)
        if k > 0:
            score_sibling(k - 1)
    score_sibling(groups - 1)

    peak = lax.fori_loop(
        0, n, lambda b, m: jnp.maximum(m, scores[b]), jnp.full((rows, rows), MASKED, jnp.float32)
    )
    peak = jnp.max(peak, axis=1, keepdims=True)
    peaks = jnp.broadcast_to(peak, (rows, rows))
    mates = prt_col[...]

    def sum_up(b, carry):
        mass, pos = carry
        s = scores[b]
        mass = mass + jnp.exp(s - peaks)
        pos = pos + jnp.where(mates == col_iota + b * rows, s, jnp.float32(0.0))
        return mass, pos

    zero = jnp.zeros((rows, rows), jnp.float32)
    mass, pos = lax.fori_loop(0, n, sum_up, (zero, zero))
    norm = peak + jnp.log(jnp.sum(mass, axis=1, keepdims=True))
    term = norm - jnp.sum(pos, axis=1, keepdims=True)
    own_col[...] = jnp.broadcast_to(norm, (rows, rows))
    norm_row = own_col[...].T
    term_row = jnp.broadcast_to(term, (rows, rows)).T
    sub = lax.broadcasted_iota(jnp.int32, (8, rows), 0)
    stats[me] = jnp.where(sub == 0, norm_row[:8], term_row[:8])
    norm_ref[...] = norm_row[:1]

    def tell(k, _):
        t = lax.rem(me + k, n)
        pltpu.make_async_remote_copy(
            src_ref=stats.at[me], dst_ref=stats.at[me],
            send_sem=barrier_free_send, recv_sem=stat_recv,
            device_id=(t // groups, lax.rem(t, groups)), device_id_type=MESH,
        ).start()
        return 0

    lax.fori_loop(1, n, tell, 0)
    everyone = stats.at[pl.ds(0, n - 1)]
    pltpu.make_async_copy(everyone, everyone, stat_recv).wait()

    per = 8
    own_norm = own_col[...]
    for j in range(0, n, per):
        def weigh(b):
            s = scores[b]
            w = jnp.exp(s - own_norm) + jnp.exp(s - stats[b, 0:1, :])
            w = w - jnp.where(mates == col_iota + b * rows, jnp.float32(2.0), jnp.float32(0.0))
            return w.astype(jnp.bfloat16)

        w = jnp.concatenate([weigh(j + i) for i in range(per)], axis=1)
        e = all_e[pl.ds(j, per)].reshape(per * rows, width)
        part = jnp.dot(w, e, preferred_element_type=jnp.float32)
        if j == 0:
            grad_ref[...] = part
        elif j + per < n:
            grad_ref[...] += part
        else:
            grad_ref[...] = (grad_ref[...] + part) * scale

    loss_ref[0, 0] = jnp.sum(stats[:, 1, :]) / (n * rows)

    for when, done in pending:
        when_do(when, done)
    pltpu.make_async_copy(everyone, everyone, barrier_free_send).wait()


def solution(mesh):
    loops, groups = mesh.shape["loop"], mesh.shape["group"]
    n = loops * groups
    half = n // 2
    ys = loops // 4

    def per_device(embeddings, partner):
        rows, width = embeddings.shape
        vmem = pl.BlockSpec(memory_space=pltpu.VMEM)
        loss, norm, grad = pl.pallas_call(
            functools.partial(kernel, loops, groups),
            out_shape=(
                jax.ShapeDtypeStruct((1, 1), jnp.float32),
                jax.ShapeDtypeStruct((1, rows), jnp.float32),
                jax.ShapeDtypeStruct((rows, width), jnp.float32),
            ),
            in_specs=[vmem, vmem],
            out_specs=(pl.BlockSpec(memory_space=pltpu.SMEM), vmem, vmem),
            scratch_shapes=[
                pltpu.VMEM((n, rows, width), jnp.bfloat16),
                pltpu.VMEM((n, rows, rows), jnp.float32),
                pltpu.VMEM((rows, rows), jnp.float32),
                pltpu.VMEM((rows, rows), jnp.int32),
                pltpu.VMEM((n, 8, rows), jnp.float32),
                pltpu.SemaphoreType.DMA((half, 2)),
                pltpu.SemaphoreType.DMA((half,)),
                pltpu.SemaphoreType.DMA((half, ys - 1)),
                pltpu.SemaphoreType.DMA((half,)),
                pltpu.SemaphoreType.DMA((half,)),
                pltpu.SemaphoreType.DMA((half, 2)),
                pltpu.SemaphoreType.DMA((half,)),
                pltpu.SemaphoreType.DMA,
                pltpu.SemaphoreType.DMA,
            ],
            compiler_params=pltpu.CompilerParams(
                collective_id=0, has_side_effects=True, vmem_limit_bytes=56 * 2**20
            ),
            cost_estimate=pl.CostEstimate(
                flops=4 * n * rows * rows * width, bytes_accessed=6 * rows * width,
                transcendentals=3 * n * rows * rows,
            ),
        )(embeddings, partner.reshape(1, rows))
        return loss.reshape(()), norm.reshape(rows), grad

    placed = (P(("loop", "group"), None), P(("loop", "group")))
    return jax.shard_map(
        per_device,
        mesh=mesh,
        in_specs=placed,
        out_specs=(P(), P(("loop", "group")), P(("loop", "group"), None)),
        check_vma=False,
    )
```

time: 387 us -> 63.9 us (0.17)
  waiting for transfers between devices: 243 us -> 0 us
  blocking collectives: 105 us -> 0 us
  Pallas kernels: 0 us -> 58.9 us
  between operations: 16 us -> 2.42 us
  matrix products: 13 us -> 0 us
    ppermute x14 -> x0, waiting for transfers between devices: 210 us -> none  [shifted(): lax.ppermute(value, axis, [(i, (i + by) % length) for i in range(length)])]
    all_gather x1 -> x0, blocking collectives: 65.5 us -> none  [per_device(): all_norms = lax.all_gather(log_norm, ('loop', 'group'), axis=0, tiled=True)]
    pallas_call x0 -> x1, Pallas kernels: none -> 58.9 us  [per_device(): pl.pallas_call(functools.partial(kernel, loops, groups), out_shape=(jax.S...]
    psum x1 -> x0, blocking collectives: 39.4 us -> none  [per_device(): loss = lax.psum(jnp.sum(log_norm - positive), ('loop', 'group')) / views]
    all_gather x1 -> x0, waiting for transfers between devices: 32.3 us -> none  [per_device(): shared = lax.all_gather(embeddings, 'group', axis=0, tiled=True)]
    dot_general x16 -> x0, matrix products: 13 us -> none  [the longest x8 7.26 us: second_update(): jnp.dot(weights.astype(jnp.bfloat16), visitor, preferred_element_type=jnp...]
  transfers between devices with their start and end apart: 15 -> 0, of which waited for: 15 -> 0; matrix products, arithmetic and copies ran while one was open for 0% -> 0% of each run, Pallas kernels for 0% -> 0%
where the time goes in v1:
time: 63.9 us; the launch traced here: 63.7 us
  Pallas kernels  58.9 us (92%)
  between operations  2.42 us (4%)
  local copies, waits for them, and re-layouts  2.4 us (4%)
    pallas_call x1, Pallas kernels, per_device(): pl.pallas_call(functools.partial(kernel, loops, groups), out_shape=(jax.S...  58.9 us
    unnamed x4, local copies, waits for them, and re-layouts  2.4 us

profile of v1, /device:TPU:0, one launch (start us, length us, event | category | flops | bytes accessed | tf_op | source)
XLA Modules:
  0.0 63.7 jit_solution(243942638245468833)
XLA Ops:
  0.6 58.9 %shard_map.49 = (f32[1,1]{1,0:T(1,128)}, f32[1,128]{1,0:T(1,128)}, f32[128,1024]{1,0:T(8,128)}) custom-call(bf16[128,1024]{1,0:T(8,128)(2,1)} %emb_ref.1, s32[1,128]{1,0:T(1,128)} %bitcast.3), custom_call_target="tpu_custom_call" | custom-call | flops 2147483648 | bytes 786432 | tf_op jit(solution)/shard_map/pallas_call | solution.py:288
  59.5 0.0 copy-start
  60.2 0.0 copy-done
  60.2 0.5 copy.9
  60.7 1.9 %copy.10 = f32[128,1024]{1,0:T(8,128)} copy(f32[128,1024]{1,0:T(8,128)} %get-tuple-element.14) | data formatting | bytes 1048576
Async XLA Ops:
  59.5 0.6 %copy-start = (f32[1,128]{1,0:T(1,128)S(1)}, f32[1,128]{1,0:T(1,128)}, u32[]{:S(2)}) copy-start(f32[1,128]{1,0:T(1,128)} %get-tuple-element.7) | copy-start | bytes 1540

commit v2 on v1

--- a/solution.py
+++ b/solution.py
@@ -14,7 +14,7 @@
 
 def kernel(
     loops, groups, emb_ref, prt_ref, loss_ref, norm_ref, grad_ref,
-    all_e, scores, own_col, prt_col, stats,
+    all_e, scores, shares, own_col, prt_col, peaks, mass, pos, stats,
     z_send, x_send, y_send, c_send, line_recv, part_recv, c_recv, barrier_free_send, stat_recv,
 ):
     l = lax.axis_index("loop")
@@ -44,16 +44,18 @@
 
     barrier = pltpu.get_barrier_semaphore()
 
-    def greet(k, _):
-        t = lax.rem(me + k, n)
-        pl.semaphore_signal(
-            barrier, inc=1, device_id=(t // groups, lax.rem(t, groups)), device_id_type=MESH
-        )
-        return 0
-
-    lax.fori_loop(1, n, greet, 0)
+    def greet(ll, gg):
+        pl.semaphore_signal(barrier, inc=1, device_id=(ll, gg), device_id_type=MESH)
+
+    greet(l + 1 - 2 * c, g)
+    greet(l + 2 - 4 * x, g)
+    for d in range(1, ys):
+        greet(lax.rem(y + d, ys) * 4 + x * 2 + c, g)
+    pl.when(g < groups - 1)(lambda: greet(l, g + 1))
+    pl.when(g > 0)(lambda: greet(l, g - 1))
     all_e[me] = emb_ref[...]
-    pl.semaphore_wait(barrier, n - 1)
+    ends = (g < groups - 1).astype(jnp.int32) + (g > 0).astype(jnp.int32)
+    pl.semaphore_wait(barrier, 1 + ys + ends)
 
     pending = []
 
@@ -98,7 +100,11 @@
         return [(g + k, g + k < groups, (-1,)), (g - k, g - k >= 0, (1,))]
 
     half = rows // 2
-    small = 16
+
+    def cuts(k):
+        if k == 0:
+            return half, rows
+        return (16 if k % 2 else 32), 48
 
     def to_z(q, z, lo, size, recv_sem, valid, steps):
         for step in steps:
@@ -117,55 +123,57 @@
             send(q, z, lo, size, y_send.at[slot(q, z), d - 1], recv_sem,
                  (lax.rem(y + d, ys) * 4 + x * 2 + c, g), valid)
 
-    def own_line(k):
+    def own_line(k, first=True, second=True):
         for z, valid, steps in sides(k):
             s = slot(mine, z)
-            if k > 0:
-                when_do(valid, lambda: arrived(mine, z, 0, rows, line_recv.at[s]))
-            to_z(mine, z, 0, rows, line_recv.at[s], valid, steps)
-            to_x(mine, z, 0, rows, line_recv.at[s], valid)
-            to_y(mine, z, 0, rows, line_recv.at[s], valid)
-            to_sibling(mine, z, valid)
+            if first:
+                if k > 0:
+                    when_do(valid, lambda: arrived(mine, z, 0, rows, line_recv.at[s]))
+                to_z(mine, z, 0, rows, line_recv.at[s], valid, steps)
+            if second:
+                to_x(mine, z, 0, rows, line_recv.at[s], valid)
+                to_y(mine, z, 0, rows, line_recv.at[s], valid)
+                to_sibling(mine, z, valid)
 
     def from_x(k):
         for z, valid, _ in sides(k):
             s = slot(other_x, z)
             when_do(valid, lambda: arrived(other_x, z, 0, rows, line_recv.at[s]))
-            to_y(other_x, z, 0, half if k == 0 else small, part_recv.at[s, 0], valid)
+            to_y(other_x, z, 0, cuts(k)[0], part_recv.at[s, 0], valid)
             to_sibling(other_x, z, valid)
 
     def from_y(k):
+        lo, hi = cuts(k)
         for z, valid, _ in sides(k):
             for q in other_y:
                 s = slot(q, z)
                 when_do(valid, lambda: arrived(q, z, 0, rows, line_recv.at[s]))
-                if k == 0:
-                    to_x(q, z, half, rows - half, part_recv.at[s, 1], valid)
-                else:
-                    to_x(q, z, small, small, part_recv.at[s, 1], valid)
+                to_x(q, z, lo, hi - lo, part_recv.at[s, 1], valid)
                 to_sibling(q, z, valid)
 
-    def from_diagonal(k):
+    def diagonal_in_plane(k):
+        lo, hi = cuts(k)
+        for z, valid, _ in sides(k):
+            for q in other_xy:
+                s = slot(q, z)
+
+                def wait_parts():
+                    arrived(q, z, 0, lo, part_recv.at[s, 0])
+                    arrived(q, z, lo, hi - lo, part_recv.at[s, 1])
+
+                when_do(valid, wait_parts)
+                if k > 0:
+                    to_sibling(q, z, valid)
+
+    def diagonal_along_z(k):
         for z, valid, steps in sides(k):
             for q in other_xy:
                 s = slot(q, z)
-
-                def wait_parts():
-                    if k == 0:
-                        arrived(q, z, 0, half, part_recv.at[s, 0])
-                        arrived(q, z, half, rows - half, part_recv.at[s, 1])
-                    else:
-                        arrived(q, z, 2 * small, rows - 2 * small, line_recv.at[s])
-
-                when_do(valid, wait_parts)
-                to_z(q, z, 2 * small, rows - 2 * small, line_recv.at[s], valid, steps)
                 if k > 0:
-                    def wait_rest():
-                        arrived(q, z, 0, small, part_recv.at[s, 0])
-                        arrived(q, z, small, small, part_recv.at[s, 1])
-
-                    when_do(valid, wait_rest)
-                to_sibling(q, z, valid)
+                    when_do(valid, lambda: arrived(q, z, 48, rows - 48, line_recv.at[s]))
+                to_z(q, z, 48, rows - 48, line_recv.at[s], valid, steps)
+                if k == 0:
+                    to_sibling(q, z, valid)
 
     row_iota = lax.broadcasted_iota(jnp.int32, (rows, rows), 0)
     col_iota = lax.broadcasted_iota(jnp.int32, (rows, rows), 1)
@@ -175,66 +183,92 @@
             emb_ref[...], all_e[b], (((1,), (1,)), ((), ())), preferred_element_type=jnp.float32
         ) * scale
         masked = jnp.logical_and(row_iota == col_iota, b == me)
-        scores[b] = jnp.where(masked, jnp.float32(MASKED), s)
-
-    def score_own(k):
+        s = jnp.where(masked, jnp.float32(MASKED), s)
+        scores[b] = s
+        old = peaks[...]
+        new = jnp.maximum(old, s)
+        mass[...] = mass[...] * jnp.exp(old - new) + jnp.exp(s - new)
+        peaks[...] = new
+        pos[...] += jnp.where(prt_col[...] == col_iota + b * rows, s, jnp.float32(0.0))
+
+    def score_own(k, quads=None):
         for z, valid, _ in sides(k):
             def run():
                 def body(q, _):
                     score(block(c, q, z))
                     return 0
-                lax.fori_loop(0, loops // 2, body, 0)
+                if quads is None:
+                    lax.fori_loop(0, loops // 2, body, 0)
+                else:
+                    for q in quads:
+                        body(q, 0)
             when_do(valid, run)
 
-    def score_sibling(k):
+    def score_sibling(k, quads=None):
         for z, valid, _ in sides(k):
             def run():
                 def body(q, _):
                     arrived(q, z, 0, rows, c_recv.at[slot(q, z)], 1 - c)
                     score(block(1 - c, q, z))
                     return 0
-                lax.fori_loop(0, loops // 2, body, 0)
+                if quads is None:
+                    lax.fori_loop(0, loops // 2, body, 0)
+                else:
+                    for q in quads:
+                        body(q, 0)
             when_do(valid, run)
 
     own_line(0)
     prt = jnp.broadcast_to(prt_ref[...].astype(jnp.float32), (rows, rows))
     prt_col[...] = prt.T.astype(jnp.int32)
+    peaks[...] = jnp.full((rows, rows), MASKED, jnp.float32)
+    mass[...] = jnp.zeros((rows, rows), jnp.float32)
+    pos[...] = jnp.zeros((rows, rows), jnp.float32)
     if groups > 1:
-        own_line(1)
-    for k in range(groups):
+        own_line(1, second=False)
+    from_x(0)
+    from_y(0)
+    diagonal_in_plane(0)
+    diagonal_along_z(0)
+    if groups > 1:
+        own_line(1, first=False)
+    if groups > 2:
+        own_line(2)
+    score_own(0)
+    for k in range(1, groups):
+        if k + 2 < groups:
+            own_line(k + 2)
+        diagonal_along_z(k)
         from_x(k)
         from_y(k)
-        if k + 2 < groups:
-            own_line(k + 2)
-        from_diagonal(k)
-        score_own(k)
-        if k > 0:
-            score_sibling(k - 1)
-    score_sibling(groups - 1)
-
-    peak = lax.fori_loop(
-        0, n, lambda b, m: jnp.maximum(m, scores[b]), jnp.full((rows, rows), MASKED, jnp.float32)
-    )
-    peak = jnp.max(peak, axis=1, keepdims=True)
-    peaks = jnp.broadcast_to(peak, (rows, rows))
+        if k > 1:
+            diagonal_in_plane(k - 1)
+            score_own(k - 1)
+        if k == 1:
+            score_sibling(0)
+        if k > 2:
+            score_sibling(k - 2)
+    last = groups - 1
+    if last > 1:
+        score_sibling(last - 1)
+    if last > 0:
+        score_own(last, (mine, other_x, *other_y))
+        score_sibling(last, (mine, other_x, *other_y))
+        diagonal_in_plane(last)
+        score_own(last, other_xy)
+        score_sibling(last, other_xy)
+    else:
+        score_sibling(last)
+
     mates = prt_col[...]
-
-    def sum_up(b, carry):
-        mass, pos = carry
-        s = scores[b]
-        mass = mass + jnp.exp(s - peaks)
-        pos = pos + jnp.where(mates == col_iota + b * rows, s, jnp.float32(0.0))
-        return mass, pos
-
-    zero = jnp.zeros((rows, rows), jnp.float32)
-    mass, pos = lax.fori_loop(0, n, sum_up, (zero, zero))
-    norm = peak + jnp.log(jnp.sum(mass, axis=1, keepdims=True))
-    term = norm - jnp.sum(pos, axis=1, keepdims=True)
+    peak = jnp.max(peaks[...], axis=1, keepdims=True)
+    norm = peak + jnp.log(jnp.sum(mass[...] * jnp.exp(peaks[...] - peak), axis=1, keepdims=True))
+    term = norm - jnp.sum(pos[...], axis=1, keepdims=True)
     own_col[...] = jnp.broadcast_to(norm, (rows, rows))
     norm_row = own_col[...].T
     term_row = jnp.broadcast_to(term, (rows, rows)).T
-    sub = lax.broadcasted_iota(jnp.int32, (8, rows), 0)
-    stats[me] = jnp.where(sub == 0, norm_row[:8], term_row[:8])
+    sub = lax.broadcasted_iota(jnp.int32, (2, rows), 0)
+    stats[me] = jnp.where(sub == 0, norm_row[:2], term_row[:2])
     norm_ref[...] = norm_row[:1]
 
     def tell(k, _):
@@ -247,17 +281,24 @@
         return 0
 
     lax.fori_loop(1, n, tell, 0)
+
+    own_norm = own_col[...]
+
+    def share(b, _):
+        mate = jnp.where(mates == col_iota + b * rows, jnp.float32(2.0), jnp.float32(0.0))
+        shares[b] = jnp.exp(scores[b] - own_norm) - mate
+        return 0
+
+    lax.fori_loop(0, n, share, 0)
+    for when, done in pending:
+        when_do(when, done)
     everyone = stats.at[pl.ds(0, n - 1)]
     pltpu.make_async_copy(everyone, everyone, stat_recv).wait()
 
     per = 8
-    own_norm = own_col[...]
     for j in range(0, n, per):
         def weigh(b):
-            s = scores[b]
-            w = jnp.exp(s - own_norm) + jnp.exp(s - stats[b, 0:1, :])
-            w = w - jnp.where(mates == col_iota + b * rows, jnp.float32(2.0), jnp.float32(0.0))
-            return w.astype(jnp.bfloat16)
+            return (shares[b] + jnp.exp(scores[b] - stats[b, 0:1, :])).astype(jnp.bfloat16)
 
         w = jnp.concatenate([weigh(j + i) for i in range(per)], axis=1)
         e = all_e[pl.ds(j, per)].reshape(per * rows, width)
@@ -271,8 +312,6 @@
 
     loss_ref[0, 0] = jnp.sum(stats[:, 1, :]) / (n * rows)
 
-    for when, done in pending:
-        when_do(when, done)
     pltpu.make_async_copy(everyone, everyone, barrier_free_send).wait()
 
 
@@ -297,9 +336,13 @@
             scratch_shapes=[
                 pltpu.VMEM((n, rows, width), jnp.bfloat16),
                 pltpu.VMEM((n, rows, rows), jnp.float32),
+                pltpu.VMEM((n, rows, rows), jnp.float32),
                 pltpu.VMEM((rows, rows), jnp.float32),
                 pltpu.VMEM((rows, rows), jnp.int32),
-                pltpu.VMEM((n, 8, rows), jnp.float32),
+                pltpu.VMEM((rows, rows), jnp.float32),
+                pltpu.VMEM((rows, rows), jnp.float32),
+                pltpu.VMEM((rows, rows), jnp.float32),
+                pltpu.VMEM((n, 2, rows), jnp.float32),
                 pltpu.SemaphoreType.DMA((half, 2)),
                 pltpu.SemaphoreType.DMA((half,)),
                 pltpu.SemaphoreType.DMA((half, ys - 1)),
@@ -311,7 +354,7 @@
                 pltpu.SemaphoreType.DMA,
             ],
             compiler_params=pltpu.CompilerParams(
-                collective_id=0, has_side_effects=True, vmem_limit_bytes=56 * 2**20
+                collective_id=0, has_side_effects=True, vmem_limit_bytes=58 * 2**20
             ),
             cost_estimate=pl.CostEstimate(
                 flops=4 * n * rows * rows * width, bytes_accessed=6 * rows * width,

time: 63.9 us -> 57.3 us (0.90)
  Pallas kernels: 58.9 us -> 52.3 us
    pallas_call x1, Pallas kernels: 58.9 us -> 52.3 us  [per_device(): pl.pallas_call(functools.partial(kernel, loops, groups), out_shape=(jax.S...]
where the time goes in v2:
time: 57.3 us; the launch traced here: 57.1 us
  Pallas kernels  52.3 us (91%)
  between operations  2.42 us (4%)
  local copies, waits for them, and re-layouts  2.4 us (4%)
    pallas_call x1, Pallas kernels, per_device(): pl.pallas_call(functools.partial(kernel, loops, groups), out_shape=(jax.S...  52.3 us
    unnamed x4, local copies, waits for them, and re-layouts  2.4 us

profile of v2, /device:TPU:0, one launch (start us, length us, event | category | flops | bytes accessed | tf_op | source)
XLA Modules:
  0.0 57.1 jit_solution(8166661437715255253)
XLA Ops:
  0.6 52.3 %shard_map.49 = (f32[1,1]{1,0:T(1,128)}, f32[1,128]{1,0:T(1,128)}, f32[128,1024]{1,0:T(8,128)}) custom-call(bf16[128,1024]{1,0:T(8,128)(2,1)} %emb_ref.1, s32[1,128]{1,0:T(1,128)} %bitcast.3), custom_call_target="tpu_custom_call" | custom-call | flops 2147483648 | bytes 786432 | tf_op jit(solution)/shard_map/pallas_call | solution.py:327
  52.9 0.0 copy-start
  53.6 0.0 copy-done
  53.6 0.5 copy.9
  54.1 1.9 %copy.10 = f32[128,1024]{1,0:T(8,128)} copy(f32[128,1024]{1,0:T(8,128)} %get-tuple-element.14) | data formatting | bytes 1048576
Async XLA Ops:
  52.9 0.6 %copy-start = (f32[1,128]{1,0:T(1,128)S(1)}, f32[1,128]{1,0:T(1,128)}, u32[]{:S(2)}) copy-start(f32[1,128]{1,0:T(1,128)} %get-tuple-element.7) | copy-start | bytes 1540

commit v3 on v2

--- a/solution.py
+++ b/solution.py
@@ -198,7 +198,7 @@
                     score(block(c, q, z))
                     return 0
                 if quads is None:
-                    lax.fori_loop(0, loops // 2, body, 0)
+                    lax.fori_loop(0, loops // 2, body, 0, unroll=4)
                 else:
                     for q in quads:
                         body(q, 0)
@@ -212,7 +212,7 @@
                     score(block(1 - c, q, z))
                     return 0
                 if quads is None:
-                    lax.fori_loop(0, loops // 2, body, 0)
+                    lax.fori_loop(0, loops // 2, body, 0, unroll=4)
                 else:
                     for q in quads:
                         body(q, 0)
@@ -229,11 +229,11 @@
     from_x(0)
     from_y(0)
     diagonal_in_plane(0)
-    diagonal_along_z(0)
     if groups > 1:
         own_line(1, first=False)
     if groups > 2:
         own_line(2)
+    diagonal_along_z(0)
     score_own(0)
     for k in range(1, groups):
         if k + 2 < groups:
@@ -271,16 +271,18 @@
     stats[me] = jnp.where(sub == 0, norm_row[:2], term_row[:2])
     norm_ref[...] = norm_row[:1]
 
-    def tell(k, _):
-        t = lax.rem(me + k, n)
-        pltpu.make_async_remote_copy(
-            src_ref=stats.at[me], dst_ref=stats.at[me],
-            send_sem=barrier_free_send, recv_sem=stat_recv,
-            device_id=(t // groups, lax.rem(t, groups)), device_id_type=MESH,
-        ).start()
-        return 0
-
-    lax.fori_loop(1, n, tell, 0)
+    def wrap(v, size):
+        return jnp.where(v >= size, v - size, v)
+
+    for dz in reversed(range(groups)):
+        for dl in range(0, loops):
+            if dz == 0 and dl == 0:
+                continue
+            pltpu.make_async_remote_copy(
+                src_ref=stats.at[me], dst_ref=stats.at[me],
+                send_sem=barrier_free_send, recv_sem=stat_recv,
+                device_id=(wrap(l + dl, loops), wrap(g + dz, groups)), device_id_type=MESH,
+            ).start()
 
     own_norm = own_col[...]
 
@@ -289,7 +291,7 @@
         shares[b] = jnp.exp(scores[b] - own_norm) - mate
         return 0
 
-    lax.fori_loop(0, n, share, 0)
+    lax.fori_loop(0, n, share, 0, unroll=4)
     for when, done in pending:
         when_do(when, done)
     everyone = stats.at[pl.ds(0, n - 1)]

time: 57.3 us -> 56.3 us (0.983)
  Pallas kernels: 52.3 us -> 51.3 us
    pallas_call x1, Pallas kernels: 52.3 us -> 51.3 us  [per_device(): pl.pallas_call(functools.partial(kernel, loops, groups), out_shape=(jax.S...]
where the time goes in v3:
time: 56.3 us; the launch traced here: 56.1 us
  Pallas kernels  51.3 us (91%)
  between operations  2.42 us (4%)
  local copies, waits for them, and re-layouts  2.4 us (4%)
    pallas_call x1, Pallas kernels, per_device(): pl.pallas_call(functools.partial(kernel, loops, groups), out_shape=(jax.S...  51.3 us
    unnamed x4, local copies, waits for them, and re-layouts  2.4 us

profile of v3, /device:TPU:0, one launch (start us, length us, event | category | flops | bytes accessed | tf_op | source)
XLA Modules:
  0.0 56.1 jit_solution(9835696111633184044)
XLA Ops:
  0.6 51.3 %shard_map.49 = (f32[1,1]{1,0:T(1,128)}, f32[1,128]{1,0:T(1,128)}, f32[128,1024]{1,0:T(8,128)}) custom-call(bf16[128,1024]{1,0:T(8,128)(2,1)} %emb_ref.1, s32[1,128]{1,0:T(1,128)} %bitcast.3), custom_call_target="tpu_custom_call" | custom-call | flops 2147483648 | bytes 786432 | tf_op jit(solution)/shard_map/pallas_call | solution.py:329
  51.9 0.0 copy-start
  52.6 0.0 copy-done
  52.6 0.5 copy.9
  53.1 1.9 %copy.10 = f32[128,1024]{1,0:T(8,128)} copy(f32[128,1024]{1,0:T(8,128)} %get-tuple-element.14) | data formatting | bytes 1048576
Async XLA Ops:
  51.9 0.6 %copy-start = (f32[1,128]{1,0:T(1,128)S(1)}, f32[1,128]{1,0:T(1,128)}, u32[]{:S(2)}) copy-start(f32[1,128]{1,0:T(1,128)} %get-tuple-element.7) | copy-start | bytes 1540
